TPU v7x, 512 devices: a whole 4x8x8 slice. The times are simulated.
512 devices in a mesh: item: 16 (over y_lo, x), cent: 32 (over z, y_hi, core).
Axes of the slice: x: 4, y: 8 (y_hi: 2, y_lo: 4; y = y_hi * 4 + y_lo), z: 8, core: 2. Of those that a mesh axis runs over, the one named last changes fastest.
Arguments:
- vectors: bfloat16 [12288, 1024], P('item'), may hold values from -256 to 256, as said below
- centroids: bfloat16 [32768, 1024], P('cent'), may hold values from -6 to 6, as said below
Outputs:
- centroids_next: bfloat16 [32768, 1024], P(('cent', 'item'))
- log_norm: float32 [12288], P('item')
Inputs may be any that keep to these rules, and one draw needn't show every extreme that they name: vectors hold finite values. `centroids`: centroid entries are independent.
All inputs are finite; a program needn't handle non-finite values.
Results may differ from a plain program's by a relative error of at most 0.0085.
Values may be sent and summed in bfloat16 or wider, within the bound.
A program may use at most 64 MiB of HBM per device.

v0:
```python
import math

import jax
import jax.numpy as jnp
from jax import lax
from jax.sharding import PartitionSpec as P

ITERS = 2


BETA = 3.0


def local_logits(vectors, rows, scale):
    raw = lax.dot_general(
        vectors, rows, (((1,), (1,)), ((), ())), preferred_element_type=jnp.float32
    )
    sqnorm = jnp.sum(jnp.square(rows.astype(jnp.float32)), axis=1)
    return scale * (raw - 0.5 * sqnorm[None, :])


def normalize(logits):
    local_peak = jnp.max(logits, axis=1)
    peak = lax.pmax(local_peak, "cent")
    expo = jnp.exp(logits - peak[:, None])
    total = lax.psum(jnp.sum(expo, axis=1), "cent")
    resp = (expo / total[:, None]).astype(jnp.bfloat16)
    return (resp, peak + jnp.log(total))


def weighted(resp, vectors):
    return lax.dot_general(
        resp, vectors, (((0,), (0,)), ((), ())), preferred_element_type=jnp.float32
    )


def update(sums, old_rows, mass):
    return ((sums + old_rows.astype(jnp.float32)) / (mass + 1.0)[:, None]).astype(jnp.bfloat16)


def shards(vectors, centroids):
    rows_per = centroids.shape[0] // lax.axis_size("item")
    offset = lax.axis_index("item") * rows_per
    scale = BETA / math.sqrt(vectors.shape[1])
    old_rows = lax.dynamic_slice_in_dim(centroids, offset, rows_per, 0)
    logits = local_logits(vectors, centroids, scale)
    result = old_rows
    log_norm = jnp.zeros((vectors.shape[0],), jnp.float32)
    for step in range(ITERS):
        resp, log_norm = normalize(logits)
        mass = lax.psum(jnp.sum(resp.astype(jnp.float32), axis=0), "item")
        own_mass = lax.dynamic_slice_in_dim(mass, offset, rows_per, 0)

        def term_rows():
            return weighted(resp, vectors)

        if step + 1 < ITERS:
            sums = lax.psum_scatter(
                term_rows().astype(jnp.bfloat16), "item", scatter_dimension=0, tiled=True
            ).astype(jnp.float32)
            fresh = update(sums, old_rows, own_mass)
            logits = local_logits(vectors, lax.all_gather(fresh, "item", axis=0, tiled=True), scale)
            old_rows = fresh
        else:
            sums = lax.psum_scatter(
                term_rows().astype(jnp.bfloat16), "item", scatter_dimension=0, tiled=True
            ).astype(jnp.float32)
            result = update(sums, old_rows, own_mass)
    return (result, log_norm)


def solution(mesh):
    in_specs = (P("item", None), P("cent", None))
    out_specs = (P(("cent", "item"), None), P("item"))
    return jax.shard_map(shards, mesh=mesh, in_specs=in_specs, out_specs=out_specs, check_vma=False)
```

profile of v0, /device:TPU:1, one launch (start us, length us, event | category | flops | bytes accessed | tf_op | source)
XLA Modules:
  0.0 644.0 jit_solution(1527836899766770282)
XLA Ops:
  7.2 2.2 multiply_reduce_fusion.1
  9.4 5.1 fusion
  14.5 91.8 %pmax.14 = f32[768]{0:T(1024)S(1)} all-reduce(f32[768]{0:T(1024)S(1)} %get-tuple-element.6), channel_id=1, replica_groups=mesh['item'=16,'cent'=32] {'cent'}, use_global_device_ids=true, to_apply=%region_2.0 | all-reduce | flops 768 | bytes 6144 | tf_op jit(solution)/shard_map/pmax | solution.py:24
  106.3 2.6 fusion.2
  108.9 91.3 %psum.28 = f32[768]{0:T(1024)S(1)} all-reduce(f32[768]{0:T(1024)S(1)} %fusion.2), channel_id=1, replica_groups=mesh['item'=16,'cent'=32] {'cent'}, use_global_device_ids=true, to_apply=%region_4.0 | all-reduce | flops 768 | bytes 6144 | tf_op jit(solution)/shard_map/psum | solution.py:26
  200.2 2.7 convert_reduce_fusion.1
  203.0 3.2 convolution_convert_fusion.1
  206.3 34.3 %psum.29 = f32[1024]{0:T(1024)S(1)} all-reduce(f32[1024]{0:T(1024)S(1)} %get-tuple-element.4), channel_id=1, replica_groups=mesh['item'=16,'cent'=32] {'item'}, use_global_device_ids=true, to_apply=%region_7.0 | all-reduce | flops 1024 | bytes 8192 | tf_op jit(solution)/shard_map/psum | solution.py:51
  240.6 0.1 dynamic-slice_add_fusion.1
  240.6 37.1 %reduce-scatter.3.cloned.1.call-done = bf16[64,1024]{1,0:T(8,128)(2,1)} async-done(((bf16[1024,1024]{1,0:T(8,128)(2,1)}), bf16[64,1024]{1,0:T(8,128)(2,1)}) %reduce-scatter.3.cloned.1.call-update) | async-done | bytes 131088 | tf_op jit(solution)/shard_map/reduce_scatter | solution.py:58
  277.7 1.7 divide_convert_fusion.3
  279.5 83.7 %all-gather.2.cloned.1.call-done = bf16[1024,1024]{1,0:T(8,128)(2,1)} async-done(((bf16[64,1024]{1,0:T(8,128)(2,1)}), bf16[1024,1024]{1,0:T(8,128)(2,1)}) %all-gather.2.cloned.1.call-update) | async-done | bytes 2097168 | tf_op jit(solution)/shard_map/all_gather | solution.py:62
  363.2 2.1 multiply_reduce_fusion
  365.3 5.1 fusion.1
  370.4 94.1 %pmax.15 = f32[768]{0:T(1024)S(1)} all-reduce(f32[768]{0:T(1024)S(1)} %get-tuple-element.8), channel_id=1, replica_groups=mesh['item'=16,'cent'=32] {'cent'}, use_global_device_ids=true, to_apply=%region_10.0 | all-reduce | flops 768 | bytes 6144 | tf_op jit(solution)/shard_map/pmax | solution.py:24
  464.5 2.6 fusion.3
  467.1 84.1 %psum.30 = f32[768]{0:T(1024)S(1)} all-reduce(f32[768]{0:T(1024)S(1)} %fusion.3), channel_id=1, replica_groups=mesh['item'=16,'cent'=32] {'cent'}, use_global_device_ids=true, to_apply=%region_12.0 | all-reduce | flops 768 | bytes 6144 | tf_op jit(solution)/shard_map/psum | solution.py:26
  551.2 2.8 convert_reduce_fusion
  554.1 3.2 convolution_convert_fusion
  557.3 35.6 %psum.31 = f32[1024]{0:T(1024)S(1)} all-reduce(f32[1024]{0:T(1024)S(1)} %get-tuple-element.2), channel_id=1, replica_groups=mesh['item'=16,'cent'=32] {'item'}, use_global_device_ids=true, to_apply=%region_15.0 | all-reduce | flops 1024 | bytes 8192 | tf_op jit(solution)/shard_map/psum | solution.py:51
  592.9 0.1 dynamic-slice_add_fusion
  593.0 0.6 log_add_fusion
  593.6 42.3 %reduce-scatter.5.cloned.1.call-done = bf16[64,1024]{1,0:T(8,128)(2,1)} async-done(((bf16[1024,1024]{1,0:T(8,128)(2,1)}), bf16[64,1024]{1,0:T(8,128)(2,1)}) %reduce-scatter.5.cloned.1.call-update) | async-done | bytes 131088 | tf_op jit(solution)/shard_map/reduce_scatter | solution.py:65
  635.8 1.6 divide_convert_fusion.2
  (12 shorter events, 0.2 us)
Async XLA Ops:
  7.2 2.3 copy-start
  7.2 270.5 %reduce-scatter.3.cloned.1.call-start = ((), (), s32[]{:S(2)}) async-start(), calls=%async_computation.2 | async-start | bytes 2228224 | tf_op jit(solution)/shard_map/reduce_scatter | solution.py:58
  206.2 157.0 %all-gather.2.cloned.1.call-start = ((), (), s32[]{:S(2)}) async-start(), calls=%async_computation.3 | async-start | bytes 2228224 | tf_op jit(solution)/shard_map/all_gather | solution.py:62
  279.4 356.4 %reduce-scatter.5.cloned.1.call-start = ((), (), s32[]{:S(2)}) async-start(), calls=%async_computation.4 | async-start | bytes 2228224 | tf_op jit(solution)/shard_map/reduce_scatter | solution.py:65
  554.1 81.8 %copy-start.1 = (bf16[64,1024]{1,0:T(8,128)(2,1)S(1)}, bf16[64,1024]{1,0:T(8,128)(2,1)}, u32[]{:S(2)}) copy-start(bf16[64,1024]{1,0:T(8,128)(2,1)} %divide_convert_fusion.3) | copy-start | bytes 393220
Sparse Core Ops, SparseCore 0:
  206.3 71.3 reduce-scatter.2
  280.3 82.7 all-gather.1
  557.4 78.4 reduce-scatter.4
where the time goes:
time: 653 us; the launch traced here: 644 us
  blocking collectives  431 us (66%)
  waiting for transfers between devices  163 us (25%)
  other arithmetic  19.2 us (3%)
  matrix products  16.5 us (3%)
  between operations  13.8 us (2%)
    pmax x2, blocking collectives, normalize(): peak = lax.pmax(local_peak, 'cent')  186 us
    psum x2, blocking collectives, normalize(): total = lax.psum(jnp.sum(expo, axis=1), 'cent')  175 us
    all_gather x1, waiting for transfers between devices, shards(): lax.all_gather(fresh, 'item', axis=0, tiled=True)  83.7 us
    reduce_scatter x2, waiting for transfers between devices, shards(): lax.psum_scatter(term_rows().astype(jnp.bfloat16), 'item', scatter_dimens...  79.3 us
    psum x2, blocking collectives, shards(): mass = lax.psum(jnp.sum(resp.astype(jnp.float32), axis=0), 'item')  69.9 us
  transfers between devices with their start and end apart: 3, of which 3 were waited for; matrix products, arithmetic and copies ran while one was open for 0% of the time, Pallas kernels for 0%

commit v1 on v0

v1 whole, which is shorter than its diff:
```python
import functools
import math

import jax
import jax.numpy as jnp
from jax import lax
from jax.experimental import pallas as pl
from jax.experimental.pallas import tpu as pltpu
from jax.sharding import PartitionSpec as P

MESH = pl.DeviceIdType.MESH
F32, BF16 = jnp.float32, jnp.bfloat16
BETA = 3.0
NX, NY, NZ, YLO = 4, 8, 8, 4
NV, D = 768, 1024
ROWS = 256
OWN = 64
NC = 4
W = D // NC
CH = 64
HALF = NV // 2
SCALE = BETA / math.sqrt(D)


def nt(a, b):
    return lax.dot_general(a, b, (((1,), (1,)), ((), ())), preferred_element_type=F32)


def merge(pairs):
    peak = functools.reduce(jnp.maximum, [p for p, _ in pairs])
    return peak, sum(t * jnp.exp(p - peak) for p, t in pairs)


def local_stats(logits):
    peak = jnp.max(logits, axis=0, keepdims=True)
    return peak, jnp.sum(jnp.exp(logits - peak), axis=0, keepdims=True)


def half_sq(rows):
    wide = rows.astype(F32)
    return 0.5 * jnp.sum(wide * wide, axis=1, keepdims=True)


def kernel(
    vec, cen, out, logn,
    vall, cvm, cnew, lbuf, resp, wbuf, rbuf, mbuf, mcol,
    core1, zst1, yst1, core2, yst2, zst2, fst2,
    in_sem, ys, yr, zs, zr, cs, cr,
    st_s, st_r, z_s, z_r, y_s, y_r, rs_s, rs_r, ag_s, ag_r, m_s, m_r,
):
    item, cent = lax.axis_index("item"), lax.axis_index("cent")
    x, q = lax.rem(item, NX), item // NX
    z, yhi, c = cent // 4, lax.rem(cent // 2, 2), lax.rem(cent, 2)
    y = yhi * YLO + q

    def dev(dx=0, dy=0, dz=0, dc=0):
        x2, y2 = lax.rem(x + dx + NX, NX), lax.rem(y + dy + NY, NY)
        z2, c2 = lax.rem(z + dz + NZ, NZ), lax.rem(c + dc, 2)
        return {"item": lax.rem(y2, YLO) * NX + x2, "cent": z2 * 4 + (y2 // YLO) * 2 + c2}

    started = []

    def send(src, dst, s, r, **to):
        copy = pltpu.make_async_remote_copy(
            src_ref=src, dst_ref=dst, send_sem=s, recv_sem=r, device_id=dev(**to), device_id_type=MESH
        )
        copy.start()
        started.append(copy)
        return copy

    mine = pl.ds(pl.multiple_of(q * NV, NV), NV)
    load_v = pltpu.make_async_copy(vec, vall.at[mine], in_sem.at[0])
    load_c = pltpu.make_async_copy(cen, cvm, in_sem.at[1])
    load_v.start()
    load_c.start()
    barrier = pltpu.get_barrier_semaphore()
    peers = [dict(dc=1)]
    peers += [dict(dx=k) for k in range(1, NX)]
    peers += [dict(dy=k) for k in range(1, NY)] + [dict(dz=k) for k in range(1, NZ)]
    for to in peers:
        pl.semaphore_signal(barrier, inc=1, device_id=dev(**to), device_id_type=MESH)
    load_v.wait()
    load_c.wait()

    def score(k, carry):
        rows = cvm[pl.ds(pl.multiple_of(k * ROWS, ROWS), ROWS), :]
        logits = SCALE * (nt(rows, vall[mine, :]) - half_sq(rows))
        return merge([carry, local_stats(logits)])

    peak, total = lax.fori_loop(
        0, 4, score, (jnp.full((1, NV), -3.0e38, F32), jnp.zeros((1, NV), F32))
    )
    core1[0, 0:1, :] = peak
    core1[0, 1:2, :] = total

    pl.semaphore_wait(barrier, len(peers))

    par = lax.rem(z, 2)
    kp, ko = 2 * par, 2 - 2 * par

    def piece(block, k):
        b = lax.rem(q + block + YLO, YLO)
        start = b * NV + c * HALF + k * CH
        return vall.at[pl.ds(pl.multiple_of(start, CH), CH)]

    def ysend(up, slot, block, k):
        side = 0 if up else 1
        part = piece(block, k)
        return send(part, part, ys.at[side, slot], yr.at[side, slot], dy=1 if up else -1)

    def zsend(up, slot, block, k):
        side = 0 if up else 1
        part = piece(block, k)
        return send(part, part, zs.at[side, slot], zr.at[side, slot], dz=1 if up else -1)

    passed = []

    def cross(block, k):
        part = piece(block, k)
        n = len(passed)
        passed.append(send(part, part, cs.at[n], cr.at[n], dc=1))

    up, down = [None] * 6, [None] * 6
    zup, zdown = [None] * 3, [None] * 3
    up[0], down[0] = ysend(True, 0, 0, kp), ysend(False, 0, 0, kp + 1)
    up[1], down[1] = ysend(True, 1, 0, kp + 1), ysend(False, 1, 0, kp)

    other = send(core1.at[0], core1.at[1], st_s.at[0], st_r.at[0], dc=1)
    other.wait_recv()
    peak, total = merge([(core1[k, 0:1, :], core1[k, 1:2, :]) for k in range(2)])
    zst1[z, 0:1, :] = peak
    zst1[z, 1:2, :] = total
    zall = [send(zst1.at[z], zst1.at[z], z_s.at[0, k], z_r.at[0, k], dz=k) for k in range(1, NZ)]

    up[0].wait_recv()
    down[0].wait_recv()
    up[2], down[2] = ysend(True, 2, -1, kp), ysend(False, 2, 1, kp + 1)
    zup[0], zdown[0] = zsend(True, 0, -1, kp), zsend(False, 0, 1, kp + 1)
    up[3], down[3] = ysend(True, 3, 0, 4), ysend(False, 3, 0, 5)
    up[4], down[4] = ysend(True, 4, 0, 5), ysend(False, 4, 0, 4)
    cross(-1, kp)
    cross(1, kp + 1)

    for copy in zall:
        copy.wait_recv()
    peak, total = merge([(zst1[k, 0:1, :], zst1[k, 1:2, :]) for k in range(NZ)])
    yst1[y, 0:1, :] = peak
    yst1[y, 1:2, :] = total
    yall = [send(yst1.at[y], yst1.at[y], y_s.at[0, k], y_r.at[0, k], dy=k) for k in range(1, NY)]

    up[1].wait_recv()
    down[1].wait_recv()
    zup[1], zdown[1] = zsend(True, 1, 1, kp), zsend(False, 1, -1, kp + 1)
    cross(-1, kp + 1)
    cross(1, kp)
    up[2].wait_recv()
    down[2].wait_recv()
    zup[2], zdown[2] = zsend(True, 2, 2, kp), zsend(False, 2, 2, kp + 1)
    cross(2, kp)
    cross(2, kp + 1)
    zup[0].wait_recv()
    zdown[0].wait_recv()
    cross(-1, ko)
    cross(1, ko + 1)
    up[3].wait_recv()
    down[3].wait_recv()
    up[5], down[5] = ysend(True, 5, -1, 4), ysend(False, 5, 1, 5)
    cross(-1, 4)
    cross(1, 5)
    zup[1].wait_recv()
    zdown[1].wait_recv()
    cross(1, ko)
    cross(-1, ko + 1)

    for copy in yall:
        copy.wait_recv()
    crow = pl.ds(pl.multiple_of(q * ROWS, ROWS), ROWS)
    rows = cvm[crow, :]
    half = half_sq(rows)

    def respond(block):
        b = lax.rem(q + block, YLO)
        peak, total = merge([(yst1[b + k, 0:1, :], yst1[b + k, 1:2, :]) for k in (0, YLO)])
        part = vall[pl.ds(pl.multiple_of(b * NV, NV), NV), :]
        logits = SCALE * (nt(rows, part) - half)
        resp[b] = (jnp.exp(logits - peak) * (1.0 / total)).astype(BF16)

    respond(0)
    up[4].wait_recv()
    down[4].wait_recv()
    cross(-1, 5)
    cross(1, 4)
    zup[2].wait_recv()
    zdown[2].wait_recv()
    cross(2, ko)
    cross(2, ko + 1)
    up[5].wait_recv()
    down[5].wait_recv()
    cross(2, 4)
    cross(2, 5)
    for copy in passed:
        copy.wait_recv()
    for block in (1, 2, 3):
        respond(block)

    own = pl.ds(pl.multiple_of(q * ROWS + x * OWN, OWN), OWN)
    own64 = pl.ds(pl.multiple_of(x * OWN, OWN), OWN)

    def reduce(it, old, emit):
        mass = sum(jnp.sum(resp[b].astype(F32), axis=1, keepdims=True) for b in range(YLO))
        mbuf[it, x] = jnp.transpose(jnp.broadcast_to(mass, (ROWS, 128)))[0:1, :]
        mall = [
            send(mbuf.at[it, x], mbuf.at[it, x], m_s.at[it, k], m_r.at[it, k], dx=k) for k in range(1, NX)
        ]
        sent = []
        for n in range(NC):
            cols = slice(n * W, (n + 1) * W)
            part = sum(
                jnp.dot(resp[b], vall[b * NV : (b + 1) * NV, cols], preferred_element_type=F32)
                for b in range(YLO)
            )
            wbuf[it, n] = part.astype(BF16).reshape(NX, OWN, W)
            rbuf[it, n, 0] = wbuf[it, n, x]
            sent.append([
                send(
                    wbuf.at[it, n, lax.rem(x + k, NX)], rbuf.at[it, n, k],
                    rs_s.at[it, n, k], rs_r.at[it, n, k], dx=k,
                )
                for k in (2, 1, 3)
            ])
        for copy in mall:
            copy.wait_recv()
        row = sum(mbuf[it, k] for k in range(NX))
        mcol[...] = jnp.transpose(jnp.broadcast_to(row, (128, ROWS)))
        div = mcol[own64, 0:1] + 1.0
        for n in range(NC):
            for copy in sent[n]:
                copy.wait_recv()
            sums = sum(rbuf[it, n, k].astype(F32) for k in range(NX))
            emit(n, ((sums + old(n).astype(F32)) / div).astype(BF16))

    gathered = []

    def spread(n, fresh):
        cnew[n, x] = fresh
        gathered.append([
            send(cnew.at[n, x], cnew.at[n, x], ag_s.at[n, k], ag_r.at[n, k], dx=k) for k in (2, 1, 3)
        ])

    reduce(0, lambda n: cvm[own, n * W : (n + 1) * W], spread)

    half = jnp.zeros((ROWS, 1), F32)
    for n in range(NC):
        for copy in gathered[n]:
            copy.wait_recv()
        rows = cnew[n].reshape(ROWS, W)
        half = half + half_sq(rows)
        for b in range(YLO):
            term = nt(rows, vall[b * NV : (b + 1) * NV, n * W : (n + 1) * W])
            lbuf[b] = term if n == 0 else lbuf[b] + term

    for b in range(YLO):
        logits = SCALE * (lbuf[b] - half)
        lbuf[b] = logits
        peak, total = local_stats(logits)
        core2[0, b, 0:1, :] = peak
        core2[0, b, 1:2, :] = total

    pair = pl.ds(2 * c, 2)
    theirs = pl.ds(2 - 2 * c, 2)
    other = send(core2.at[0, theirs], core2.at[1, theirs], st_s.at[1], st_r.at[1], dc=1)
    other.wait_recv()
    for j in range(2):
        b = 2 * c + j
        peak, total = merge([(core2[k, b, 0:1, :], core2[k, b, 1:2, :]) for k in range(2)])
        yst2[y, j, 0:1, :] = peak
        yst2[y, j, 1:2, :] = total
    yall = [send(yst2.at[y], yst2.at[y], y_s.at[1, k], y_r.at[1, k], dy=k) for k in range(1, NY)]
    for copy in yall:
        copy.wait_recv()
    for j in range(2):
        peak, total = merge([(yst2[k, j, 0:1, :], yst2[k, j, 1:2, :]) for k in range(NY)])
        zst2[z, j, 0:1, :] = peak
        zst2[z, j, 1:2, :] = total
    zall = [send(zst2.at[z], zst2.at[z], z_s.at[1, k], z_r.at[1, k], dz=k) for k in range(1, NZ)]
    for copy in zall:
        copy.wait_recv()
    for j in range(2):
        peak, total = merge([(zst2[k, j, 0:1, :], zst2[k, j, 1:2, :]) for k in range(NZ)])
        fst2[2 * c + j, 0:1, :] = peak
        fst2[2 * c + j, 1:2, :] = total
    other = send(fst2.at[pair], fst2.at[pair], st_s.at[2], st_r.at[2], dc=1)
    other.wait_recv()

    for b in range(YLO):
        peak, total = fst2[b, 0:1, :], fst2[b, 1:2, :]
        resp[b] = (jnp.exp(lbuf[b] - peak) * (1.0 / total)).astype(BF16)
    norm = fst2[q, 0:1, :] + jnp.log(fst2[q, 1:2, :])
    for k in range(NV // 128):
        logn[k : k + 1, :] = norm[:, k * 128 : (k + 1) * 128]

    def finish(n, fresh):
        out[:, n * W : (n + 1) * W] = fresh

    reduce(1, lambda n: cnew[n, x], finish)

    for copy in started:
        copy.wait_send()


def shards(vectors, centroids):
    dma = pltpu.SemaphoreType.DMA
    result, log_norm = pl.pallas_call(
        kernel,
        out_shape=(
            jax.ShapeDtypeStruct((OWN, D), BF16),
            jax.ShapeDtypeStruct((NV // 128, 128), F32),
        ),
        in_specs=[pl.BlockSpec(memory_space=pl.ANY)] * 2,
        out_specs=(pl.BlockSpec(memory_space=pltpu.VMEM),) * 2,
        scratch_shapes=[
            pltpu.VMEM((YLO * NV, D), BF16),
            pltpu.VMEM((4 * ROWS, D), BF16),
            pltpu.VMEM((NC, NX, OWN, W), BF16),
            pltpu.VMEM((YLO, ROWS, NV), F32),
            pltpu.VMEM((YLO, ROWS, NV), BF16),
            pltpu.VMEM((2, NC, NX, OWN, W), BF16),
            pltpu.VMEM((2, NC, NX, OWN, W), BF16),
            pltpu.VMEM((2, NX, 1, ROWS), F32),
            pltpu.VMEM((ROWS, 128), F32),
            pltpu.VMEM((2, 2, NV), F32),
            pltpu.VMEM((NZ, 2, NV), F32),
            pltpu.VMEM((NY, 2, NV), F32),
            pltpu.VMEM((2, YLO, 2, NV), F32),
            pltpu.VMEM((NY, 2, 2, NV), F32),
            pltpu.VMEM((NZ, 2, 2, NV), F32),
            pltpu.VMEM((YLO, 2, NV), F32),
            dma((2,)),
            dma((2, 6)), dma((2, 6)), dma((2, 3)), dma((2, 3)), dma((18,)), dma((18,)),
            dma((3,)), dma((3,)), dma((2, NZ)), dma((2, NZ)), dma((2, NY)), dma((2, NY)),
            dma((2, NC, NX)), dma((2, NC, NX)), dma((NC, NX)), dma((NC, NX)),
            dma((2, NX)), dma((2, NX)),
        ],
        compiler_params=pltpu.CompilerParams(
            collective_id=0, has_side_effects=True, vmem_limit_bytes=48 * 2**20
        ),
    )(vectors, centroids)
    return result, log_norm.reshape(NV)


def solution(mesh):
    in_specs = (P("item", None), P("cent", None))
    out_specs = (P(("cent", "item"), None), P("item"))
    return jax.shard_map(shards, mesh=mesh, in_specs=in_specs, out_specs=out_specs, check_vma=False)
```

time: 653 us -> 82.8 us (0.13); the launches traced: 644 us -> 82.7 us
  blocking collectives: 431 us -> 0 us
  waiting for transfers between devices: 163 us -> 0 us
  Pallas kernels: 0 us -> 77.8 us
  other arithmetic: 19.2 us -> 0 us
  matrix products: 16.5 us -> 0 us
  between operations: 13.8 us -> 0.65 us
    psum x4 -> x0, blocking collectives: 245 us -> none  [the longest x2 175 us: normalize(): total = lax.psum(jnp.sum(expo, axis=1), 'cent')]
    pmax x2 -> x0, blocking collectives: 186 us -> none  [normalize(): peak = lax.pmax(local_peak, 'cent')]
    all_gather x1 -> x0, waiting for transfers between devices: 83.7 us -> none  [shards(): lax.all_gather(fresh, 'item', axis=0, tiled=True)]
    reduce_scatter x2 -> x0, waiting for transfers between devices: 79.3 us -> none  [shards(): lax.psum_scatter(term_rows().astype(jnp.bfloat16), 'item', scatter_dimens...]
    pallas_call x0 -> x1, Pallas kernels: none -> 77.8 us  [shards(): pl.pallas_call(kernel, out_shape=(jax.ShapeDtypeStruct((OWN, D), BF16), j...]
    dot_general x4 -> x0, matrix products: 16.5 us -> none  [the longest x2 10.2 us: local_logits(): lax.dot_general(vectors, rows, (((1,), (1,)), ((), ())), preferred_elemen...]
    reduce_sum x6 -> x0, other arithmetic: 15 us -> none  [the longest x2 5.57 us: shards(): mass = lax.psum(jnp.sum(resp.astype(jnp.float32), axis=0), 'item')]
  transfers between devices with their start and end apart: 3 -> 0, of which waited for: 3 -> 0; matrix products, arithmetic and copies ran while one was open for 0% -> 0% of each run, Pallas kernels for 0% -> 0%
where the time goes in v1:
time: 82.8 us; the launch traced here: 82.7 us
  Pallas kernels  77.8 us (94%)
  local copies, waits for them, and re-layouts  4.24 us (5%)
    pallas_call x1, Pallas kernels, shards(): pl.pallas_call(kernel, out_shape=(jax.ShapeDtypeStruct((OWN, D), BF16), j...  77.8 us
    unnamed x6, local copies, waits for them, and re-layouts  4.24 us

profile of v1, /device:TPU:1, one launch (start us, length us, event | category | flops | bytes accessed | tf_op | source)
XLA Modules:
  0.0 82.7 jit_solution(12753148100289246351)
XLA Ops:
  0.6 0.0 copy-start
  0.6 1.6 %copy-done = bf16[1024,1024]{1,0:T(8,128)(2,1)S(1)} copy-done((bf16[1024,1024]{1,0:T(8,128)(2,1)S(1)}, bf16[1024,1024]{1,0:T(8,128)(2,1)}, u32[]{:S(2)}) %copy-start) | copy-done | bytes 2097176
  2.2 0.0 copy-start.1
  2.2 1.4 %copy-done.1 = bf16[768,1024]{1,0:T(8,128)(2,1)S(1)} copy-done((bf16[768,1024]{1,0:T(8,128)(2,1)S(1)}, bf16[768,1024]{1,0:T(8,128)(2,1)}, u32[]{:S(2)}) %copy-start.1) | copy-done | bytes 1572888
  3.6 77.8 %shard_map.41 = (bf16[64,1024]{1,0:T(8,128)(2,1)S(1)}, f32[6,128]{1,0:T(8,128)S(1)}) custom-call(bf16[768,1024]{1,0:T(8,128)(2,1)S(1)} %copy-done.1, bf16[1024,1024]{1,0:T(8,128)(2,1)S(1)} %copy-done), custom_call_target="tpu_custom_call" | custom-call | tf_op jit(solution)/shard_map/pallas_call | solution.py:313
  81.4 0.7 copy.6
  82.1 0.6 copy.7
Async XLA Ops:
  0.6 1.6 %copy-start = (bf16[1024,1024]{1,0:T(8,128)(2,1)S(1)}, bf16[1024,1024]{1,0:T(8,128)(2,1)}, u32[]{:S(2)}) copy-start(bf16[1024,1024]{1,0:T(8,128)(2,1)} %cen.1) | copy-start | bytes 6291460
  2.2 1.4 %copy-start.1 = (bf16[768,1024]{1,0:T(8,128)(2,1)S(1)}, bf16[768,1024]{1,0:T(8,128)(2,1)}, u32[]{:S(2)}) copy-start(bf16[768,1024]{1,0:T(8,128)(2,1)} %vec.1) | copy-start | bytes 4718596

commit v2 on v1

v2 whole, which is shorter than its diff:
```python
import functools
import math

import jax
import jax.numpy as jnp
from jax import lax
from jax.experimental import pallas as pl
from jax.experimental.pallas import tpu as pltpu
from jax.sharding import PartitionSpec as P

MESH = pl.DeviceIdType.MESH
F32, BF16 = jnp.float32, jnp.bfloat16
BETA = 3.0
NX, NY, NZ, YLO = 4, 8, 8, 4
NV, D = 768, 1024
ROWS = 256
OWN = 64
NC = 4
W = D // NC
HALF = NV // 2
PART, REST = 80, 32
GATHER = 2 * (3 * PART + 3 * REST + 3 * PART) + 3 * HALF
SEMS = 47
SCALE = BETA / math.sqrt(D)


def nt(a, b):
    return lax.dot_general(a, b, (((1,), (1,)), ((), ())), preferred_element_type=F32)


def merge(pairs):
    peak = functools.reduce(jnp.maximum, [p for p, _ in pairs])
    return peak, sum(t * jnp.exp(p - peak) for p, t in pairs)


def local_stats(logits):
    peak = jnp.max(logits, axis=0, keepdims=True)
    return peak, jnp.sum(jnp.exp(logits - peak), axis=0, keepdims=True)


def half_sq(rows):
    wide = rows.astype(F32)
    return 0.5 * jnp.sum(wide * wide, axis=1, keepdims=True)


def kernel(
    vec, cen, out, logn,
    vall, cvm, cnew, lbuf, resp, wbuf, rbuf, mbuf, mcol,
    core1, zst1, yst1, core2, st2, fst2, sem,
):
    item, cent = lax.axis_index("item"), lax.axis_index("cent")
    x, q = lax.rem(item, NX), item // NX
    z, yhi, c = cent // 4, lax.rem(cent // 2, 2), lax.rem(cent, 2)
    y = yhi * YLO + q
    names = {}

    def sem_of(name):
        return sem.at[names.setdefault(name, len(names))]

    def dev(dx=0, dy=0, dz=0, dc=0):
        x2, y2 = lax.rem(x + dx + NX, NX), lax.rem(y + dy + NY, NY)
        z2, c2 = lax.rem(z + dz + NZ, NZ), lax.rem(c + dc, 2)
        return {"item": lax.rem(y2, YLO) * NX + x2, "cent": z2 * 4 + (y2 // YLO) * 2 + c2}

    def send(src, dst, group, arrived, **to):
        pltpu.make_async_remote_copy(
            src_ref=src, dst_ref=dst, send_sem=sem_of("s" + group), recv_sem=sem_of("r" + arrived),
            device_id=dev(**to), device_id_type=MESH,
        ).start()

    def wait(like, name):
        pltpu.make_async_copy(like, like, sem_of(name)).wait()

    barrier = pltpu.get_barrier_semaphore()
    peers = [dict(dc=1)]
    peers += [dict(dy=k) for k in range(1, NY)] + [dict(dz=k) for k in range(1, NZ)]
    peers += [dict(dx=k) for k in range(1, NX)]
    for to in peers:
        pl.semaphore_signal(barrier, inc=1, device_id=dev(**to), device_id_type=MESH)
    mine = pl.ds(pl.multiple_of(q * NV, NV), NV)
    load_v = pltpu.make_async_copy(vec, vall.at[mine], sem_of("load_v"))
    load_c = pltpu.make_async_copy(cen, cvm, sem_of("load_c"))
    load_v.start()
    load_c.start()
    pl.semaphore_wait(barrier, len(peers))

    par = lax.rem(z, 2)

    def rows_of(kind, high):
        if kind == "rest":
            return c * HALF + 4 * PART + high * REST, REST
        share = par if kind == "own" else 1 - par
        return c * HALF + (2 * share + high) * PART, PART

    def piece(block, kind, high):
        start, n = rows_of(kind, high)
        b = lax.rem(q + block + YLO, YLO)
        return vall.at[pl.ds(pl.multiple_of(b * NV + start, 16), n)]

    def first(kind, high, arrived, **to):
        start, n = rows_of(kind, high)
        send(vec.at[pl.ds(pl.multiple_of(start, 16), n)], piece(0, kind, high), "gather", arrived, **to)

    def along(block, kind, high, arrived, **to):
        part = piece(block, kind, high)
        send(part, part, "gather", arrived, **to)

    def cross(block, kind, high):
        along(block, kind, high, "far" if block == 2 else "near", dc=1)

    def landed(n, name):
        wait(vall.at[pl.ds(0, n)], name)

    first("own", 0, "A", dy=1)
    first("own", 1, "A", dy=-1)
    first("own", 1, "B", dy=1)
    first("own", 0, "B", dy=-1)
    load_v.wait()
    load_c.wait()

    def score(k, carry):
        rows = cvm[pl.ds(pl.multiple_of(k * ROWS, ROWS), ROWS), :]
        logits = SCALE * (nt(rows, vall[mine, :]) - half_sq(rows))
        lbuf[k] = logits
        return merge([carry, local_stats(logits)])

    peak, total = lax.fori_loop(
        0, 4, score, (jnp.full((1, NV), -3.0e38, F32), jnp.zeros((1, NV), F32))
    )
    core1[0, 0:1, :] = peak
    core1[0, 1:2, :] = total
    send(core1.at[0], core1.at[1], "core1", "core1", dc=1)
    wait(core1.at[1], "rcore1")
    peak, total = merge([(core1[k, 0:1, :], core1[k, 1:2, :]) for k in range(2)])
    zst1[z, 0:1, :] = peak
    zst1[z, 1:2, :] = total
    for k in range(1, NZ):
        send(zst1.at[z], zst1.at[z], "zst", "zst", dz=k)

    landed(2 * PART, "rA")
    along(-1, "own", 0, "F", dy=1)
    along(1, "own", 1, "F", dy=-1)
    along(-1, "own", 0, "Z0", dz=1)
    along(1, "own", 1, "Z0", dz=-1)
    first("rest", 0, "C", dy=1)
    first("rest", 1, "C", dy=-1)
    first("rest", 1, "D", dy=1)
    first("rest", 0, "D", dy=-1)
    cross(-1, "own", 0)
    cross(1, "own", 1)
    landed(2 * PART, "rB")
    along(1, "own", 0, "Z1", dz=1)
    along(-1, "own", 1, "Z1", dz=-1)
    cross(-1, "own", 1)
    cross(1, "own", 0)

    wait(zst1.at[pl.ds(0, NZ - 1)], "rzst")
    peak, total = merge([(zst1[k, 0:1, :], zst1[k, 1:2, :]) for k in range(NZ)])
    yst1[y, 0:1, :] = peak
    yst1[y, 1:2, :] = total
    for k in range(1, NY):
        send(yst1.at[y], yst1.at[y], "yst", "yst", dy=k)

    landed(2 * PART, "rF")
    along(2, "own", 0, "Z2", dz=1)
    along(2, "own", 1, "Z2", dz=-1)
    cross(2, "own", 0)
    cross(2, "own", 1)
    landed(2 * PART, "rZ0")
    cross(-1, "other", 0)
    cross(1, "other", 1)
    landed(2 * REST, "rC")
    along(-1, "rest", 0, "G", dy=1)
    along(1, "rest", 1, "G", dy=-1)
    cross(-1, "rest", 0)
    cross(1, "rest", 1)
    landed(2 * PART, "rZ1")
    cross(1, "other", 0)
    cross(-1, "other", 1)
    landed(2 * REST, "rD")
    cross(-1, "rest", 1)
    cross(1, "rest", 0)

    crow = pl.ds(pl.multiple_of(q * ROWS, ROWS), ROWS)
    half = half_sq(cvm[crow, :])

    def respond(block):
        b = lax.rem(q + block, YLO)
        peak, total = merge([(yst1[b + k, 0:1, :], yst1[b + k, 1:2, :]) for k in (0, YLO)])
        if block == 0:
            logits = lbuf[q]
        else:
            part = vall[pl.ds(pl.multiple_of(b * NV, NV), NV), :]
            logits = SCALE * (nt(cvm[crow, :], part) - half)
        resp[b] = (jnp.exp(logits - peak) * (1.0 / total)).astype(BF16)

    wait(yst1.at[pl.ds(0, NY - 1)], "ryst")
    respond(0)
    landed(2 * REST, "rG")
    cross(2, "rest", 0)
    cross(2, "rest", 1)
    landed(2 * HALF, "rnear")
    respond(3)
    landed(2 * PART, "rZ2")
    cross(2, "other", 0)
    cross(2, "other", 1)
    respond(1)
    landed(HALF, "rfar")
    respond(2)

    own = pl.ds(pl.multiple_of(q * ROWS + x * OWN, OWN), OWN)
    own64 = pl.ds(pl.multiple_of(x * OWN, OWN), OWN)

    def reduce(it, old, emit):
        for n in range(NC):
            cols = slice(n * W, (n + 1) * W)
            part = sum(
                jnp.dot(resp[b], vall[b * NV : (b + 1) * NV, cols], preferred_element_type=F32)
                for b in range(YLO)
            )
            wbuf[it, n] = part.astype(BF16).reshape(NX, OWN, W)
            rbuf[it, n, 0] = wbuf[it, n, x]
            for k in (2, 1, 3):
                send(
                    wbuf.at[it, n, lax.rem(x + k, NX)], rbuf.at[it, n, k],
                    f"rs{it}", f"rs{it}{n}", dx=k,
                )
            if n == 0:
                mass = sum(jnp.sum(resp[b].astype(F32), axis=1, keepdims=True) for b in range(YLO))
                mbuf[it, x] = jnp.transpose(jnp.broadcast_to(mass, (ROWS, 128)))[0:1, :]
                for k in range(1, NX):
                    send(mbuf.at[it, x], mbuf.at[it, x], f"m{it}", f"m{it}", dx=k)
        wait(mbuf.at[it, pl.ds(0, NX - 1)], f"rm{it}")
        row = sum(mbuf[it, k] for k in range(NX))
        mcol[...] = jnp.transpose(jnp.broadcast_to(row, (128, ROWS)))
        div = mcol[own64, 0:1] + 1.0
        for n in range(NC):
            wait(rbuf.at[it, n, pl.ds(1, NX - 1)], f"rrs{it}{n}")
            sums = sum(rbuf[it, n, k].astype(F32) for k in range(NX))
            emit(n, ((sums + old(n).astype(F32)) / div).astype(BF16))

    def spread(n, fresh):
        cnew[n, x] = fresh
        for k in (2, 1, 3):
            send(cnew.at[n, x], cnew.at[n, x], "ag", f"ag{n}", dx=k)

    reduce(0, lambda n: cvm[own, n * W : (n + 1) * W], spread)

    half = jnp.zeros((ROWS, 1), F32)
    for n in range(NC):
        wait(cnew.at[n, pl.ds(0, NX - 1)], f"rag{n}")
        rows = cnew[n].reshape(ROWS, W)
        half = half + half_sq(rows)
        for b in range(YLO):
            term = nt(rows, vall[b * NV : (b + 1) * NV, n * W : (n + 1) * W])
            if n > 0:
                term = lbuf[b] + term
            if n < NC - 1:
                lbuf[b] = term
            else:
                logits = SCALE * (term - half)
                peak = jnp.max(logits, axis=0, keepdims=True)
                expo = jnp.exp(logits - peak)
                lbuf[b] = expo
                core2[0, b, 0:1, :] = peak
                core2[0, b, 1:2, :] = jnp.sum(expo, axis=0, keepdims=True)

    theirs = pl.ds(2 - 2 * c, 2)
    pair = pl.ds(2 * c, 2)
    send(core2.at[0, theirs], core2.at[1, theirs], "core2", "core2", dc=1)
    wait(core2.at[1, pair], "rcore2")
    found = [
        merge([(core2[k, 2 * c + j, 0:1, :], core2[k, 2 * c + j, 1:2, :]) for k in range(2)]) for j in range(2)
    ]
    for s in range(2):
        turn = lax.rem(c + s, 2)
        at = y * (1 - turn) + z * turn
        for j in range(2):
            st2[s, at, j, 0:1, :], st2[s, at, j, 1:2, :] = found[j]
        for k in range(1, NY):
            send(st2.at[s, at], st2.at[s, at], f"st{s}", f"st{s}", dy=k * (1 - turn), dz=k * turn)
        wait(st2.at[s, pl.ds(0, NY - 1)], f"rst{s}")
        found = [merge([(st2[s, k, j, 0:1, :], st2[s, k, j, 1:2, :]) for k in range(NY)]) for j in range(2)]
    for j in range(2):
        fst2[2 * c + j, 0:1, :], fst2[2 * c + j, 1:2, :] = found[j]
    send(fst2.at[pair], fst2.at[pair], "core3", "core3", dc=1)
    wait(fst2.at[theirs], "rcore3")

    for b in range(YLO):
        peak, total = fst2[b, 0:1, :], fst2[b, 1:2, :]
        share = jnp.exp(core2[0, b, 0:1, :] - peak) * (1.0 / total)
        resp[b] = (lbuf[b] * share).astype(BF16)

    def finish(n, fresh):
        out[:, n * W : (n + 1) * W] = fresh

    reduce(1, lambda n: cnew[n, x], finish)
    norm = fst2[q, 0:1, :] + jnp.log(fst2[q, 1:2, :])
    for k in range(NV // 128):
        logn[k : k + 1, :] = norm[:, k * 128 : (k + 1) * 128]

    landed(GATHER, "sgather")
    wait(core1.at[0], "score1")
    wait(zst1.at[pl.ds(0, NZ - 1)], "szst")
    wait(yst1.at[pl.ds(0, NY - 1)], "syst")
    for it in range(2):
        wait(rbuf.at[it, pl.ds(0, NX - 1)], f"srs{it}")
        wait(mbuf.at[it, pl.ds(0, NX - 1)], f"sm{it}")
        wait(st2.at[it, pl.ds(0, NY - 1)], f"sst{it}")
    wait(cnew.at[pl.ds(0, NX - 1)], "sag")
    wait(core2.at[0, pair], "score2")
    wait(fst2.at[pair], "score3")
    assert len(names) == SEMS, len(names)


def shards(vectors, centroids):
    result, log_norm = pl.pallas_call(
        kernel,
        out_shape=(
            jax.ShapeDtypeStruct((OWN, D), BF16),
            jax.ShapeDtypeStruct((NV // 128, 128), F32),
        ),
        in_specs=[pl.BlockSpec(memory_space=pl.ANY)] * 2,
        out_specs=(pl.BlockSpec(memory_space=pltpu.VMEM),) * 2,
        scratch_shapes=[
            pltpu.VMEM((YLO * NV, D), BF16),
            pltpu.VMEM((4 * ROWS, D), BF16),
            pltpu.VMEM((NC, NX, OWN, W), BF16),
            pltpu.VMEM((YLO, ROWS, NV), F32),
            pltpu.VMEM((YLO, ROWS, NV), BF16),
            pltpu.VMEM((2, NC, NX, OWN, W), BF16),
            pltpu.VMEM((2, NC, NX, OWN, W), BF16),
            pltpu.VMEM((2, NX, 1, ROWS), F32),
            pltpu.VMEM((ROWS, 128), F32),
            pltpu.VMEM((2, 2, NV), F32),
            pltpu.VMEM((NZ, 2, NV), F32),
            pltpu.VMEM((NY, 2, NV), F32),
            pltpu.VMEM((2, YLO, 2, NV), F32),
            pltpu.VMEM((2, NY, 2, 2, NV), F32),
            pltpu.VMEM((YLO, 2, NV), F32),
            pltpu.SemaphoreType.DMA((SEMS,)),
        ],
        compiler_params=pltpu.CompilerParams(
            collective_id=0, has_side_effects=True, vmem_limit_bytes=54272 * 2**10
        ),
    )(vectors, centroids)
    return result, log_norm.reshape(NV)


def solution(mesh):
    in_specs = (P("item", None), P("cent", None))
    out_specs = (P(("cent", "item"), None), P("item"))
    return jax.shard_map(shards, mesh=mesh, in_specs=in_specs, out_specs=out_specs, check_vma=False)
```

time: 82.8 us -> 76.3 us (0.921)
  Pallas kernels: 77.8 us -> 74.3 us
  local copies, waits for them, and re-layouts: 4.24 us -> 1.25 us
    pallas_call x1, Pallas kernels: 77.8 us -> 74.3 us  [shards(): pl.pallas_call(kernel, out_shape=(jax.ShapeDtypeStruct((OWN, D), BF16), j...]
    unnamed x6 -> x2, local copies, waits for them, and re-layouts: 4.24 us -> 1.25 us
where the time goes in v2:
time: 76.3 us; the launch traced here: 76.2 us
  Pallas kernels  74.3 us (97%)
  local copies, waits for them, and re-layouts  1.25 us (2%)
    pallas_call x1, Pallas kernels, shards(): pl.pallas_call(kernel, out_shape=(jax.ShapeDtypeStruct((OWN, D), BF16), j...  74.3 us

profile of v2, /device:TPU:1, one launch (start us, length us, event | category | flops | bytes accessed | tf_op | source)
XLA Modules:
  0.0 76.2 jit_solution(7411737471230297806)
XLA Ops:
  0.6 74.3 %shard_map.41 = (bf16[64,1024]{1,0:T(8,128)(2,1)S(1)}, f32[6,128]{1,0:T(8,128)S(1)}) custom-call(bf16[768,1024]{1,0:T(8,128)(2,1)} %vec.1, bf16[1024,1024]{1,0:T(8,128)(2,1)} %cen.1), custom_call_target="tpu_custom_call" | custom-call | tf_op jit(solution)/shard_map/pallas_call | solution.py:317
  74.9 0.7 copy.6
  75.6 0.6 copy.7

commit v3 on v2

--- a/solution.py
+++ b/solution.py
@@ -18,9 +18,11 @@
 NC = 4
 W = D // NC
 HALF = NV // 2
+STEPS = 48, 32
 PART, REST = 80, 32
 GATHER = 2 * (3 * PART + 3 * REST + 3 * PART) + 3 * HALF
-SEMS = 47
+SEMS = 49
+FARTHEST = (4, 3, 5, 2, 6, 1, 7)
 SCALE = BETA / math.sqrt(D)
 
 
@@ -46,7 +48,7 @@
 def kernel(
     vec, cen, out, logn,
     vall, cvm, cnew, lbuf, resp, wbuf, rbuf, mbuf, mcol,
-    core1, zst1, yst1, core2, st2, fst2, sem,
+    core1, zst1, yst1, core2, st2, fst2, sem, ready,
 ):
     item, cent = lax.axis_index("item"), lax.axis_index("cent")
     x, q = lax.rem(item, NX), item // NX
@@ -57,7 +59,17 @@
     def sem_of(name):
         return sem.at[names.setdefault(name, len(names))]
 
-    def dev(dx=0, dy=0, dz=0, dc=0):
+    ids = {}
+
+    def dev(**to):
+        if not all(isinstance(step, int) for step in to.values()):
+            return dev_of(**to)
+        key = tuple(to.items())
+        if key not in ids:
+            ids[key] = dev_of(**to)
+        return ids[key]
+
+    def dev_of(dx=0, dy=0, dz=0, dc=0):
         x2, y2 = lax.rem(x + dx + NX, NX), lax.rem(y + dy + NY, NY)
         z2, c2 = lax.rem(z + dz + NZ, NZ), lax.rem(c + dc, 2)
         return {"item": lax.rem(y2, YLO) * NX + x2, "cent": z2 * 4 + (y2 // YLO) * 2 + c2}
@@ -72,21 +84,28 @@
         pltpu.make_async_copy(like, like, sem_of(name)).wait()
 
     barrier = pltpu.get_barrier_semaphore()
-    peers = [dict(dc=1)]
-    peers += [dict(dy=k) for k in range(1, NY)] + [dict(dz=k) for k in range(1, NZ)]
-    peers += [dict(dx=k) for k in range(1, NX)]
-    for to in peers:
-        pl.semaphore_signal(barrier, inc=1, device_id=dev(**to), device_id_type=MESH)
+    around = [dict(dy=1), dict(dy=-1), dict(dz=1), dict(dz=-1), dict(dx=1), dict(dx=-1)]
+    beyond = [dict(dy=2), dict(dy=-2), dict(dz=2), dict(dz=-2)]
+
+    def tell(semaphore, peers):
+        for to in peers:
+            pl.semaphore_signal(semaphore, inc=1, device_id=dev(**to), device_id_type=MESH)
+
+    tell(barrier, [dict(dc=1)] + around)
     mine = pl.ds(pl.multiple_of(q * NV, NV), NV)
     load_v = pltpu.make_async_copy(vec, vall.at[mine], sem_of("load_v"))
     load_c = pltpu.make_async_copy(cen, cvm, sem_of("load_c"))
     load_v.start()
     load_c.start()
-    pl.semaphore_wait(barrier, len(peers))
+    pl.semaphore_wait(barrier, 1 + len(around))
+    tell(ready.at[0], around)
 
     par = lax.rem(z, 2)
 
     def rows_of(kind, high):
+        if isinstance(kind, tuple):
+            start, _ = rows_of(kind[0], high)
+            return start + kind[1] * STEPS[0], STEPS[kind[1]]
         if kind == "rest":
             return c * HALF + 4 * PART + high * REST, REST
         share = par if kind == "own" else 1 - par
@@ -115,6 +134,8 @@
     first("own", 1, "A", dy=-1)
     first("own", 1, "B", dy=1)
     first("own", 0, "B", dy=-1)
+    first("rest", 0, "C", dy=1)
+    first("rest", 1, "C", dy=-1)
     load_v.wait()
     load_c.wait()
 
@@ -124,9 +145,11 @@
         lbuf[k] = logits
         return merge([carry, local_stats(logits)])
 
-    peak, total = lax.fori_loop(
-        0, 4, score, (jnp.full((1, NV), -3.0e38, F32), jnp.zeros((1, NV), F32))
-    )
+    carry = jnp.full((1, NV), -3.0e38, F32), jnp.zeros((1, NV), F32)
+    carry = lax.fori_loop(0, 2, score, carry)
+    pl.semaphore_wait(ready.at[0], len(around))
+    tell(ready.at[1], beyond)
+    peak, total = lax.fori_loop(2, 4, score, carry)
     core1[0, 0:1, :] = peak
     core1[0, 1:2, :] = total
     send(core1.at[0], core1.at[1], "core1", "core1", dc=1)
@@ -134,16 +157,16 @@
     peak, total = merge([(core1[k, 0:1, :], core1[k, 1:2, :]) for k in range(2)])
     zst1[z, 0:1, :] = peak
     zst1[z, 1:2, :] = total
-    for k in range(1, NZ):
+    pl.semaphore_wait(ready.at[1], len(beyond))
+    for k in FARTHEST:
         send(zst1.at[z], zst1.at[z], "zst", "zst", dz=k)
 
     landed(2 * PART, "rA")
-    along(-1, "own", 0, "F", dy=1)
-    along(1, "own", 1, "F", dy=-1)
+    for h in range(2):
+        along(-1, ("own", h), 0, f"F{h}", dy=1)
+        along(1, ("own", h), 1, f"F{h}", dy=-1)
     along(-1, "own", 0, "Z0", dz=1)
     along(1, "own", 1, "Z0", dz=-1)
-    first("rest", 0, "C", dy=1)
-    first("rest", 1, "C", dy=-1)
     first("rest", 1, "D", dy=1)
     first("rest", 0, "D", dy=-1)
     cross(-1, "own", 0)
@@ -158,12 +181,13 @@
     peak, total = merge([(zst1[k, 0:1, :], zst1[k, 1:2, :]) for k in range(NZ)])
     yst1[y, 0:1, :] = peak
     yst1[y, 1:2, :] = total
-    for k in range(1, NY):
+    for k in FARTHEST:
         send(yst1.at[y], yst1.at[y], "yst", "yst", dy=k)
 
-    landed(2 * PART, "rF")
-    along(2, "own", 0, "Z2", dz=1)
-    along(2, "own", 1, "Z2", dz=-1)
+    for h in range(2):
+        landed(2 * STEPS[h], f"rF{h}")
+        along(2, ("own", h), 0, f"Y{h}", dz=1)
+        along(2, ("own", h), 1, f"Y{h}", dz=-1)
     cross(2, "own", 0)
     cross(2, "own", 1)
     landed(2 * PART, "rZ0")
@@ -196,14 +220,17 @@
 
     wait(yst1.at[pl.ds(0, NY - 1)], "ryst")
     respond(0)
+    landed(2 * STEPS[0], "rY0")
+    cross(2, ("other", 0), 0)
+    cross(2, ("other", 0), 1)
+    landed(2 * HALF, "rnear")
+    respond(3)
+    landed(2 * STEPS[1], "rY1")
+    cross(2, ("other", 1), 0)
+    cross(2, ("other", 1), 1)
     landed(2 * REST, "rG")
     cross(2, "rest", 0)
     cross(2, "rest", 1)
-    landed(2 * HALF, "rnear")
-    respond(3)
-    landed(2 * PART, "rZ2")
-    cross(2, "other", 0)
-    cross(2, "other", 1)
     respond(1)
     landed(HALF, "rfar")
     respond(2)
@@ -277,7 +304,7 @@
         at = y * (1 - turn) + z * turn
         for j in range(2):
             st2[s, at, j, 0:1, :], st2[s, at, j, 1:2, :] = found[j]
-        for k in range(1, NY):
+        for k in FARTHEST:
             send(st2.at[s, at], st2.at[s, at], f"st{s}", f"st{s}", dy=k * (1 - turn), dz=k * turn)
         wait(st2.at[s, pl.ds(0, NY - 1)], f"rst{s}")
         found = [merge([(st2[s, k, j, 0:1, :], st2[s, k, j, 1:2, :]) for k in range(NY)]) for j in range(2)]
@@ -339,6 +366,7 @@
             pltpu.VMEM((2, NY, 2, 2, NV), F32),
             pltpu.VMEM((YLO, 2, NV), F32),
             pltpu.SemaphoreType.DMA((SEMS,)),
+            pltpu.SemaphoreType.REGULAR((2,)),
         ],
         compiler_params=pltpu.CompilerParams(
             collective_id=0, has_side_effects=True, vmem_limit_bytes=54272 * 2**10

time: 76.3 us -> 73.9 us (0.969)
  Pallas kernels: 74.3 us -> 71.9 us
    pallas_call x1, Pallas kernels: 74.3 us -> 71.9 us  [shards(): pl.pallas_call(kernel, out_shape=(jax.ShapeDtypeStruct((OWN, D), BF16), j...]
where the time goes in v3:
time: 73.9 us; the launch traced here: 73.8 us
  Pallas kernels  71.9 us (97%)
  local copies, waits for them, and re-layouts  1.25 us (2%)
    pallas_call x1, Pallas kernels, shards(): pl.pallas_call(kernel, out_shape=(jax.ShapeDtypeStruct((OWN, D), BF16), j...  71.9 us

profile of v3, /device:TPU:1, one launch (start us, length us, event | category | flops | bytes accessed | tf_op | source)
XLA Modules:
  0.0 73.8 jit_solution(1760371045288378027)
XLA Ops:
  0.6 71.9 %shard_map.41 = (bf16[64,1024]{1,0:T(8,128)(2,1)S(1)}, f32[6,128]{1,0:T(8,128)S(1)}) custom-call(bf16[768,1024]{1,0:T(8,128)(2,1)} %vec.1, bf16[1024,1024]{1,0:T(8,128)(2,1)} %cen.1), custom_call_target="tpu_custom_call" | custom-call | tf_op jit(solution)/shard_map/pallas_call | solution.py:344
  72.5 0.7 copy.6
  73.2 0.6 copy.7

commit v4 on v3

--- a/solution.py
+++ b/solution.py
@@ -274,12 +274,16 @@
     reduce(0, lambda n: cvm[own, n * W : (n + 1) * W], spread)
 
     half = jnp.zeros((ROWS, 1), F32)
+    theirs = pl.ds(2 - 2 * c, 2)
+    pair = pl.ds(2 * c, 2)
     for n in range(NC):
         wait(cnew.at[n, pl.ds(0, NX - 1)], f"rag{n}")
         rows = cnew[n].reshape(ROWS, W)
         half = half + half_sq(rows)
-        for b in range(YLO):
-            term = nt(rows, vall[b * NV : (b + 1) * NV, n * W : (n + 1) * W])
+        for i in range(YLO):
+            b = i if n < NC - 1 else lax.rem(2 - 2 * c + i, YLO)
+            start = b * NV if n < NC - 1 else pl.multiple_of(b * NV, NV)
+            term = nt(rows, vall[pl.ds(start, NV), n * W : (n + 1) * W])
             if n > 0:
                 term = lbuf[b] + term
             if n < NC - 1:
@@ -291,10 +295,9 @@
                 lbuf[b] = expo
                 core2[0, b, 0:1, :] = peak
                 core2[0, b, 1:2, :] = jnp.sum(expo, axis=0, keepdims=True)
-
-    theirs = pl.ds(2 - 2 * c, 2)
-    pair = pl.ds(2 * c, 2)
-    send(core2.at[0, theirs], core2.at[1, theirs], "core2", "core2", dc=1)
+                if i == 1:
+                    send(core2.at[0, theirs], core2.at[1, theirs], "core2", "core2", dc=1)
+
     wait(core2.at[1, pair], "rcore2")
     found = [
         merge([(core2[k, 2 * c + j, 0:1, :], core2[k, 2 * c + j, 1:2, :]) for k in range(2)]) for j in range(2)
@@ -311,9 +314,11 @@
     for j in range(2):
         fst2[2 * c + j, 0:1, :], fst2[2 * c + j, 1:2, :] = found[j]
     send(fst2.at[pair], fst2.at[pair], "core3", "core3", dc=1)
-    wait(fst2.at[theirs], "rcore3")
-
-    for b in range(YLO):
+
+    for i in range(YLO):
+        if i == 2:
+            wait(fst2.at[theirs], "rcore3")
+        b = lax.rem(2 * c + i, YLO)
         peak, total = fst2[b, 0:1, :], fst2[b, 1:2, :]
         share = jnp.exp(core2[0, b, 0:1, :] - peak) * (1.0 / total)
         resp[b] = (lbuf[b] * share).astype(BF16)

time: 73.9 us -> 73.8 us (level)
  no operation moved by 1% of the time
where the time goes in v4:
time: 73.8 us; the launch traced here: 73.7 us
  Pallas kernels  71.8 us (97%)
  local copies, waits for them, and re-layouts  1.25 us (2%)
    pallas_call x1, Pallas kernels, shards(): pl.pallas_call(kernel, out_shape=(jax.ShapeDtypeStruct((OWN, D), BF16), j...  71.8 us

profile of v4, /device:TPU:1, one launch (start us, length us, event | category | flops | bytes accessed | tf_op | source)
XLA Modules:
  0.0 73.7 jit_solution(10375697740773185657)
XLA Ops:
  0.6 71.8 %shard_map.41 = (bf16[64,1024]{1,0:T(8,128)(2,1)S(1)}, f32[6,128]{1,0:T(8,128)S(1)}) custom-call(bf16[768,1024]{1,0:T(8,128)(2,1)} %vec.1, bf16[1024,1024]{1,0:T(8,128)(2,1)} %cen.1), custom_call_target="tpu_custom_call" | custom-call | tf_op jit(solution)/shard_map/pallas_call | solution.py:349
  72.4 0.7 copy.6
  73.1 0.6 copy.7

commit v5 on v4

--- a/solution.py
+++ b/solution.py
@@ -35,6 +35,11 @@
     return peak, sum(t * jnp.exp(p - peak) for p, t in pairs)
 
 
+def rows_at(b):
+    start = b * NV
+    return pl.ds(start if isinstance(b, int) else pl.multiple_of(start, NV), NV)
+
+
 def local_stats(logits):
     peak = jnp.max(logits, axis=0, keepdims=True)
     return peak, jnp.sum(jnp.exp(logits - peak), axis=0, keepdims=True)
@@ -47,7 +52,7 @@
 
 def kernel(
     vec, cen, out, logn,
-    vall, cvm, cnew, lbuf, resp, wbuf, rbuf, mbuf, mcol,
+    vall, cvm, cnew, lbuf, resp, acc, wbuf, rbuf, mbuf, mcol,
     core1, zst1, yst1, core2, st2, fst2, sem, ready,
 ):
     item, cent = lax.axis_index("item"), lax.axis_index("cent")
@@ -232,19 +237,24 @@
     cross(2, "rest", 0)
     cross(2, "rest", 1)
     respond(1)
+
+    def weigh(b, n):
+        part = vall[rows_at(b), n * W : (n + 1) * W]
+        return jnp.dot(resp[b], part, preferred_element_type=F32)
+
+    acc[...] = sum(weigh(lax.rem(q + k, YLO), 0) for k in (0, 3, 1))
     landed(HALF, "rfar")
     respond(2)
 
     own = pl.ds(pl.multiple_of(q * ROWS + x * OWN, OWN), OWN)
     own64 = pl.ds(pl.multiple_of(x * OWN, OWN), OWN)
 
-    def reduce(it, old, emit):
+    def reduce(it, late, old, emit):
         for n in range(NC):
-            cols = slice(n * W, (n + 1) * W)
-            part = sum(
-                jnp.dot(resp[b], vall[b * NV : (b + 1) * NV, cols], preferred_element_type=F32)
-                for b in range(YLO)
-            )
+            if n == 0:
+                part = acc[...] + sum(weigh(b, 0) for b in late)
+            else:
+                part = sum(weigh(b, n) for b in range(YLO))
             wbuf[it, n] = part.astype(BF16).reshape(NX, OWN, W)
             rbuf[it, n, 0] = wbuf[it, n, x]
             for k in (2, 1, 3):
@@ -271,7 +281,7 @@
         for k in (2, 1, 3):
             send(cnew.at[n, x], cnew.at[n, x], "ag", f"ag{n}", dx=k)
 
-    reduce(0, lambda n: cvm[own, n * W : (n + 1) * W], spread)
+    reduce(0, [lax.rem(q + 2, YLO)], lambda n: cvm[own, n * W : (n + 1) * W], spread)
 
     half = jnp.zeros((ROWS, 1), F32)
     theirs = pl.ds(2 - 2 * c, 2)
@@ -315,10 +325,11 @@
         fst2[2 * c + j, 0:1, :], fst2[2 * c + j, 1:2, :] = found[j]
     send(fst2.at[pair], fst2.at[pair], "core3", "core3", dc=1)
 
-    for i in range(YLO):
-        if i == 2:
+    others = [2 - 2 * c, 3 - 2 * c]
+    for b in [2 * c, 2 * c + 1, *others]:
+        if b is others[0]:
+            acc[...] = weigh(2 * c, 0) + weigh(2 * c + 1, 0)
             wait(fst2.at[theirs], "rcore3")
-        b = lax.rem(2 * c + i, YLO)
         peak, total = fst2[b, 0:1, :], fst2[b, 1:2, :]
         share = jnp.exp(core2[0, b, 0:1, :] - peak) * (1.0 / total)
         resp[b] = (lbuf[b] * share).astype(BF16)
@@ -326,7 +337,7 @@
     def finish(n, fresh):
         out[:, n * W : (n + 1) * W] = fresh
 
-    reduce(1, lambda n: cnew[n, x], finish)
+    reduce(1, others, lambda n: cnew[n, x], finish)
     norm = fst2[q, 0:1, :] + jnp.log(fst2[q, 1:2, :])
     for k in range(NV // 128):
         logn[k : k + 1, :] = norm[:, k * 128 : (k + 1) * 128]
@@ -360,6 +371,7 @@
             pltpu.VMEM((NC, NX, OWN, W), BF16),
             pltpu.VMEM((YLO, ROWS, NV), F32),
             pltpu.VMEM((YLO, ROWS, NV), BF16),
+            pltpu.VMEM((ROWS, W), F32),
             pltpu.VMEM((2, NC, NX, OWN, W), BF16),
             pltpu.VMEM((2, NC, NX, OWN, W), BF16),
             pltpu.VMEM((2, NX, 1, ROWS), F32),

time: 73.8 us -> 73.5 us (level)
  no operation moved by 1% of the time
where the time goes in v5:
time: 73.5 us; the launch traced here: 73.4 us
  Pallas kernels  71.5 us (97%)
  local copies, waits for them, and re-layouts  1.25 us (2%)
    pallas_call x1, Pallas kernels, shards(): pl.pallas_call(kernel, out_shape=(jax.ShapeDtypeStruct((OWN, D), BF16), j...  71.5 us

profile of v5, /device:TPU:1, one launch (start us, length us, event | category | flops | bytes accessed | tf_op | source)
XLA Modules:
  0.0 73.4 jit_solution(9655766534426789648)
XLA Ops:
  0.6 71.5 %shard_map.41 = (bf16[64,1024]{1,0:T(8,128)(2,1)S(1)}, f32[6,128]{1,0:T(8,128)S(1)}) custom-call(bf16[768,1024]{1,0:T(8,128)(2,1)} %vec.1, bf16[1024,1024]{1,0:T(8,128)(2,1)} %cen.1), custom_call_target="tpu_custom_call" | custom-call | tf_op jit(solution)/shard_map/pallas_call | solution.py:360
  72.2 0.7 copy.6
  72.8 0.6 copy.7

commit v6 on v5

--- a/solution.py
+++ b/solution.py
@@ -103,7 +103,6 @@
     load_v.start()
     load_c.start()
     pl.semaphore_wait(barrier, 1 + len(around))
-    tell(ready.at[0], around)
 
     par = lax.rem(z, 2)
 
@@ -141,6 +140,7 @@
     first("own", 0, "B", dy=-1)
     first("rest", 0, "C", dy=1)
     first("rest", 1, "C", dy=-1)
+    tell(ready.at[0], around)
     load_v.wait()
     load_c.wait()
 
@@ -158,14 +158,6 @@
     core1[0, 0:1, :] = peak
     core1[0, 1:2, :] = total
     send(core1.at[0], core1.at[1], "core1", "core1", dc=1)
-    wait(core1.at[1], "rcore1")
-    peak, total = merge([(core1[k, 0:1, :], core1[k, 1:2, :]) for k in range(2)])
-    zst1[z, 0:1, :] = peak
-    zst1[z, 1:2, :] = total
-    pl.semaphore_wait(ready.at[1], len(beyond))
-    for k in FARTHEST:
-        send(zst1.at[z], zst1.at[z], "zst", "zst", dz=k)
-
     landed(2 * PART, "rA")
     for h in range(2):
         along(-1, ("own", h), 0, f"F{h}", dy=1)
@@ -176,6 +168,14 @@
     first("rest", 0, "D", dy=-1)
     cross(-1, "own", 0)
     cross(1, "own", 1)
+    wait(core1.at[1], "rcore1")
+    peak, total = merge([(core1[k, 0:1, :], core1[k, 1:2, :]) for k in range(2)])
+    zst1[z, 0:1, :] = peak
+    zst1[z, 1:2, :] = total
+    pl.semaphore_wait(ready.at[1], len(beyond))
+    for k in FARTHEST:
+        send(zst1.at[z], zst1.at[z], "zst", "zst", dz=k)
+
     landed(2 * PART, "rB")
     along(1, "own", 0, "Z1", dz=1)
     along(-1, "own", 1, "Z1", dz=-1)

time: 73.5 us -> 73.9 us (level)
  no operation moved by 1% of the time
where the time goes in v6:
time: 73.9 us; the launch traced here: 73.8 us
  Pallas kernels  71.9 us (97%)
  local copies, waits for them, and re-layouts  1.25 us (2%)
    pallas_call x1, Pallas kernels, shards(): pl.pallas_call(kernel, out_shape=(jax.ShapeDtypeStruct((OWN, D), BF16), j...  71.9 us

profile of v6, /device:TPU:1, one launch (start us, length us, event | category | flops | bytes accessed | tf_op | source)
XLA Modules:
  0.0 73.8 jit_solution(6401974423006642762)
XLA Ops:
  0.6 71.9 %shard_map.41 = (bf16[64,1024]{1,0:T(8,128)(2,1)S(1)}, f32[6,128]{1,0:T(8,128)S(1)}) custom-call(bf16[768,1024]{1,0:T(8,128)(2,1)} %vec.1, bf16[1024,1024]{1,0:T(8,128)(2,1)} %cen.1), custom_call_target="tpu_custom_call" | custom-call | tf_op jit(solution)/shard_map/pallas_call | solution.py:360
  72.5 0.7 copy.6
  73.2 0.6 copy.7

commit v7 on v5

--- a/solution.py
+++ b/solution.py
@@ -249,7 +249,7 @@
     own = pl.ds(pl.multiple_of(q * ROWS + x * OWN, OWN), OWN)
     own64 = pl.ds(pl.multiple_of(x * OWN, OWN), OWN)
 
-    def reduce(it, late, old, emit):
+    def reduce(it, late, old, emit, meanwhile=None):
         for n in range(NC):
             if n == 0:
                 part = acc[...] + sum(weigh(b, 0) for b in late)
@@ -267,6 +267,8 @@
                 mbuf[it, x] = jnp.transpose(jnp.broadcast_to(mass, (ROWS, 128)))[0:1, :]
                 for k in range(1, NX):
                     send(mbuf.at[it, x], mbuf.at[it, x], f"m{it}", f"m{it}", dx=k)
+        if meanwhile is not None:
+            meanwhile()
         wait(mbuf.at[it, pl.ds(0, NX - 1)], f"rm{it}")
         row = sum(mbuf[it, k] for k in range(NX))
         mcol[...] = jnp.transpose(jnp.broadcast_to(row, (128, ROWS)))
@@ -337,22 +339,27 @@
     def finish(n, fresh):
         out[:, n * W : (n + 1) * W] = fresh
 
-    reduce(1, others, lambda n: cnew[n, x], finish)
-    norm = fst2[q, 0:1, :] + jnp.log(fst2[q, 1:2, :])
-    for k in range(NV // 128):
-        logn[k : k + 1, :] = norm[:, k * 128 : (k + 1) * 128]
-
-    landed(GATHER, "sgather")
-    wait(core1.at[0], "score1")
-    wait(zst1.at[pl.ds(0, NZ - 1)], "szst")
-    wait(yst1.at[pl.ds(0, NY - 1)], "syst")
-    for it in range(2):
+    def left(it):
         wait(rbuf.at[it, pl.ds(0, NX - 1)], f"srs{it}")
         wait(mbuf.at[it, pl.ds(0, NX - 1)], f"sm{it}")
-        wait(st2.at[it, pl.ds(0, NY - 1)], f"sst{it}")
-    wait(cnew.at[pl.ds(0, NX - 1)], "sag")
-    wait(core2.at[0, pair], "score2")
-    wait(fst2.at[pair], "score3")
+
+    def close():
+        norm = fst2[q, 0:1, :] + jnp.log(fst2[q, 1:2, :])
+        for k in range(NV // 128):
+            logn[k : k + 1, :] = norm[:, k * 128 : (k + 1) * 128]
+        landed(GATHER, "sgather")
+        wait(core1.at[0], "score1")
+        wait(zst1.at[pl.ds(0, NZ - 1)], "szst")
+        wait(yst1.at[pl.ds(0, NY - 1)], "syst")
+        for k in range(2):
+            wait(st2.at[k, pl.ds(0, NY - 1)], f"sst{k}")
+        wait(cnew.at[pl.ds(0, NX - 1)], "sag")
+        wait(core2.at[0, pair], "score2")
+        wait(fst2.at[pair], "score3")
+        left(0)
+
+    reduce(1, others, lambda n: cnew[n, x], finish, close)
+    left(1)
     assert len(names) == SEMS, len(names)
 
 

time: 73.5 us -> 73.5 us (level)
  no operation moved by 1% of the time
where the time goes in v7:
time: 73.5 us; the launch traced here: 73.4 us
  Pallas kernels  71.5 us (97%)
  local copies, waits for them, and re-layouts  1.25 us (2%)
    pallas_call x1, Pallas kernels, shards(): pl.pallas_call(kernel, out_shape=(jax.ShapeDtypeStruct((OWN, D), BF16), j...  71.5 us

profile of v7, /device:TPU:1, one launch (start us, length us, event | category | flops | bytes accessed | tf_op | source)
XLA Modules:
  0.0 73.4 jit_solution(2739246937728842945)
XLA Ops:
  0.6 71.5 %shard_map.41 = (bf16[64,1024]{1,0:T(8,128)(2,1)S(1)}, f32[6,128]{1,0:T(8,128)S(1)}) custom-call(bf16[768,1024]{1,0:T(8,128)(2,1)} %vec.1, bf16[1024,1024]{1,0:T(8,128)(2,1)} %cen.1), custom_call_target="tpu_custom_call" | custom-call | tf_op jit(solution)/shard_map/pallas_call | solution.py:367
  72.1 0.7 copy.6
  72.8 0.6 copy.7
